TPU v7x, 256 devices: a whole 4x4x8 slice. The times are simulated.
256 devices in a mesh: grp: 8 (over z), seq: 16 (over y, x), resp: 2 (over core).
Axes of the slice: x: 4, y: 4, z: 8, core: 2. Of those that a mesh axis runs over, the one named last changes fastest.
Arguments:
- prompt_xbc: bfloat16 [65536, 5376], P(('grp', 'seq', 'resp')), parts along dimension 0, may hold values from -6 to 6
- prompt_z: bfloat16 [65536, 5120], P(('grp', 'seq', 'resp')), parts along dimension 0, may hold values from -6 to 6
- prompt_step: float32 [80, 65536], P(None, ('grp', 'seq', 'resp')), parts along dimension 1, may hold values from 0 to 0.2
- prompt_keep: float32 [80, 65536], P(None, ('grp', 'seq', 'resp')), parts along dimension 1, may hold values from -0.6 to 0
- resp_xbc: bfloat16 [256, 128, 5376], P(('grp', 'seq', 'resp')), parts along dimension 0, may hold values from -6 to 6
- resp_z: bfloat16 [256, 128, 5120], P(('grp', 'seq', 'resp')), parts along dimension 0, may hold values from -6 to 6
- resp_step: float32 [80, 256, 128], P(None, ('grp', 'seq', 'resp')), parts along dimension 1, may hold values from 0 to 0.2
- resp_keep: float32 [80, 256, 128], P(None, ('grp', 'seq', 'resp')), parts along dimension 1, may hold values from -0.6 to 0
- resp_len: int32 [256], P(('grp', 'seq', 'resp')), parts along dimension 0, may hold values from 32 to 128, as said below
- conv_weight: float32 [4, 5376], replicated, may hold values from -3 to 3
- conv_bias: float32 [5376], replicated, may hold values from -3 to 3
- skip: float32 [80], replicated, may hold values from 0.5 to 1.5
- gain: float32 [5120], replicated, may hold values from 0.25 to 1.75
Outputs:
- prompt_out: bfloat16 [65536, 5120], P(('grp', 'seq', 'resp')), parts along dimension 0
- resp_out: bfloat16 [256, 128, 5120], P(('grp', 'seq', 'resp')), parts along dimension 0
There are 8 independent parts, one for each index of `grp`. A program takes and returns all parts, laid end to end along the dimension named above; an argument that names none is the same for every part. Nothing has to cross between parts.
Inputs may be any that keep to these rules, and one draw needn't show every extreme that they name: `resp_len`: some response fills all 128 positions.
All inputs are finite; a program needn't handle non-finite values.
Results may differ from a plain program's by a relative error of at most 0.0034.
Values may be sent and summed in bfloat16 or wider, within the bound.
No kernel may reach another device: no remote copies, remote signals or barrier semaphores. Data moves between devices by JAX's collectives and lax.ppermute only.
A program may use at most 256 MiB of HBM per device.

v0:
```python
import jax
import jax.numpy as jnp
from jax import lax
from jax.sharding import PartitionSpec as P

HEADS = 80
HEAD_DIM = 64
STATE = 128
KERNEL = 4
BLOCK = 128
D_INNER = 5120
EPS = 1e-05


def shifted(shard, axis, by):
    count = lax.axis_size(axis)
    pairs = [(i, i + by) for i in range(count) if 0 <= i + by < count]
    return lax.ppermute(shard, axis, pairs)


def prefix(value, axis, join, neutral):
    count, mine = (lax.axis_size(axis), lax.axis_index(axis))
    pieces = jax.tree.map(lambda part: lax.all_gather(part, axis), value)
    running = jax.tree.map(
        lambda part, zero: jnp.full_like(part, 0) + jnp.asarray(zero, part.dtype), value, neutral
    )

    def lap(position, running):
        longer = join(running, jax.tree.map(lambda part: part[position], pieces))
        return jax.tree.map(lambda new, old: jnp.where(position < mine, new, old), longer, running)

    return lax.fori_loop(0, count - 1, lap, running)


def from_root(block, axis, source):
    block = jnp.where(lax.axis_index(axis) == source, block, jnp.zeros_like(block))
    return lax.psum(block, axis)


def conv_silu(input_rows, history, conv_weight, conv_bias):
    row_count = input_rows.shape[0]
    padded = jnp.concatenate([history, input_rows], axis=0).astype(jnp.float32)
    conv_total = jnp.broadcast_to(conv_bias[None, :], (row_count, conv_bias.shape[0]))
    for offset in range(KERNEL):
        conv_total = conv_total + conv_weight[offset][None, :] * padded[offset : offset + row_count]
    return jax.nn.silu(conv_total).astype(jnp.bfloat16)


def block_local(activations, step_rows, keep_rows, want_state):
    row_count = activations.shape[0]
    values = activations[:, :D_INNER].reshape(row_count, HEADS, HEAD_DIM)
    key_rows = activations[:, D_INNER : D_INNER + STATE]
    queries = activations[:, D_INNER + STATE :]
    log_cum = jnp.cumsum(keep_rows, axis=1)
    scores = jnp.dot(queries, key_rows.T, preferred_element_type=jnp.float32)
    token_places = jnp.arange(row_count)
    causal = token_places[:, None] >= token_places[None, :]
    row_factor = jnp.exp(log_cum)
    col_factor = jnp.exp(-log_cum) * step_rows
    product_rows = row_factor[:, :, None] * scores[None] * col_factor[:, None, :]
    mixing = jnp.where(causal[None], product_rows, 0.0).astype(jnp.bfloat16)
    within = jnp.einsum("hts,shp->thp", mixing, values, preferred_element_type=jnp.float32)
    added_state = None
    if want_state:
        tail_weight = jnp.exp(log_cum[:, -1:] - log_cum) * step_rows
        weighted = (values.astype(jnp.float32) * tail_weight.T[:, :, None]).astype(jnp.bfloat16)
        added_state = jnp.einsum(
            "thp,tn->hpn", weighted, key_rows, preferred_element_type=jnp.float32
        )
    return (within, added_state, log_cum)


def carried(queries, carry_state, log_cum):
    carried_part = jnp.einsum(
        "tn,hpn->thp",
        queries,
        carry_state,
        precision=lax.Precision.HIGHEST,
        preferred_element_type=jnp.float32,
    )
    return carried_part * jnp.exp(log_cum).T[:, :, None]


def run_device(activations, step_rows, keep_rows, block, want_state):
    row_count = activations.shape[0]
    block_count = row_count // block
    queries = activations[:, D_INNER + STATE :].astype(jnp.float32)
    block_outs = []
    carry_state = None
    for index in range(block_count):
        row_start = index * block
        needed = want_state or index + 1 < block_count
        within, added_state, log_cum = block_local(
            activations[row_start : row_start + block],
            step_rows[:, row_start : row_start + block],
            keep_rows[:, row_start : row_start + block],
            needed,
        )
        if carry_state is not None:
            within = within + carried(queries[row_start : row_start + block], carry_state, log_cum)
            carry_state = jnp.exp(log_cum[:, -1])[:, None, None] * carry_state + added_state
        else:
            carry_state = added_state
        block_outs.append(within)
    return (jnp.concatenate(block_outs, axis=0), carry_state)


def finish(pre_norm, activations, gate_rows, skip, gain):
    row_count = pre_norm.shape[0]
    values = activations[:, :D_INNER].astype(jnp.float32).reshape(row_count, HEADS, HEAD_DIM)
    mixed_sum = (pre_norm + skip[None, :, None] * values).reshape(row_count, D_INNER)
    gated_rows = mixed_sum * jax.nn.silu(gate_rows.astype(jnp.float32))
    inv_rms = lax.rsqrt(jnp.mean(gated_rows * gated_rows, axis=1, keepdims=True) + EPS)
    return (gated_rows * inv_rms * gain[None, :]).astype(jnp.bfloat16)


def compose(earlier, latter):
    return (earlier[0] * latter[0], latter[0][:, None, None] * earlier[1] + latter[1])


def shards(
    prompt_xbc,
    prompt_z,
    prompt_step,
    prompt_keep,
    resp_xbc,
    resp_z,
    resp_step,
    resp_keep,
    resp_len,
    conv_weight,
    conv_bias,
    skip,
    gain,
):
    device_count = lax.axis_size(("seq", "resp"))
    own_rows = prompt_xbc[prompt_xbc.shape[0] - (KERNEL - 1) :]
    history = shifted(own_rows, ("seq", "resp"), 1)
    prompt_acts = conv_silu(prompt_xbc, history, conv_weight, conv_bias)
    within, local_state = run_device(prompt_acts, prompt_step, prompt_keep, BLOCK, True)
    running = jnp.cumsum(prompt_keep, axis=1)
    through = jnp.exp(running[:, -1])
    identity = (jnp.ones_like(through), jnp.zeros_like(local_state))
    before, entering = prefix((through, local_state), ("seq", "resp"), compose, identity)
    queries = prompt_acts[:, D_INNER + STATE :].astype(jnp.float32)
    pre_norm = within + carried(queries, entering, running)
    prompt_out = finish(pre_norm, prompt_acts, prompt_z, skip, gain)
    ending = through[:, None, None] * entering + local_state
    final_state, tail_wide = (
        from_root(ending, ("seq", "resp"), device_count - 1),
        from_root(own_rows.astype(jnp.float32), ("seq", "resp"), device_count - 1),
    )
    last_rows = tail_wide.astype(jnp.bfloat16)
    resp_positions = resp_xbc.shape[1]
    response_block = min(BLOCK, resp_positions)
    token_places = jnp.arange(resp_positions)

    def respond(pieces):
        input_rows, gate_rows, step_rows, keep_rows, length = pieces
        activations = conv_silu(input_rows, last_rows, conv_weight, conv_bias)
        within_resp, unused = run_device(activations, step_rows, keep_rows, response_block, False)
        resp_running = jnp.cumsum(keep_rows, axis=1)
        resp_queries = activations[:, D_INNER + STATE :].astype(jnp.float32)
        pre_resp = within_resp + carried(resp_queries, final_state, resp_running)
        finished = finish(pre_resp, activations, gate_rows, skip, gain)
        return jnp.where((token_places < length)[:, None], finished, jnp.zeros_like(finished))

    resp_out = lax.map(
        respond,
        (
            resp_xbc,
            resp_z,
            jnp.transpose(resp_step, (1, 0, 2)),
            jnp.transpose(resp_keep, (1, 0, 2)),
            resp_len,
        ),
    )
    return (prompt_out, resp_out)


def solution(mesh):
    return jax.shard_map(
        shards,
        mesh=mesh,
        in_specs=(
            P(("grp", "seq", "resp"), None),
            P(("grp", "seq", "resp"), None),
            P(None, ("grp", "seq", "resp")),
            P(None, ("grp", "seq", "resp")),
            P(("grp", "seq", "resp"), None, None),
            P(("grp", "seq", "resp"), None, None),
            P(None, ("grp", "seq", "resp"), None),
            P(None, ("grp", "seq", "resp"), None),
            P(("grp", "seq", "resp")),
            P(),
            P(),
            P(),
            P(),
        ),
        out_specs=(P(("grp", "seq", "resp"), None), P(("grp", "seq", "resp"), None, None)),
        check_vma=False,
    )
```

profile of v0, /device:TPU:6, one launch (start us, length us, event | category | flops | bytes accessed | tf_op | source)
XLA Modules:
  0.0 508.1 jit_solution(13911984617777442369)
XLA Ops:
  16.5 3.5 multiply_convert_fusion
  22.0 2.4 copy.63
  24.4 2.4 copy.64
  36.8 115.3 %all-reduce.1 = (f32[2560]{0:T(1024)S(1)}, bf16[3,5376]{1,0:T(4,128)(2,1)S(1)}) all-reduce(f32[2560]{0:T(1024)S(1)} %dynamic-update-slice, f32[3,5376]{1,0:T(4,128)S(1)} %convert_select_fusion), channel_id=2, replica_groups=mesh['grp'=8,'seq'=16,'resp'=2] {'seq','resp'}, use_global_device_ids=true, to_apply=%add | all-reduce | flops 18688 | bytes 117248
  158.0 2.4 copy.73
  160.7 2.9 copy.78
  165.4 4.7 slice_convert_fusion
  170.0 6.4 %copy.71 = f32[256,5120]{0,1:T(8,128)} copy(f32[256,5120]{1,0:T(8,128)} %slice_convert_fusion) | data formatting | bytes 10485760 | tf_op jit(solution)/shard_map/reshape | solution.py:110
  178.3 4.0 fusion.15
  182.3 3.6 fusion.33
  185.9 3.6 bitcast_add_fusion.2
  189.5 96.8 %all-gather.4.cloned.1.call-done = f32[2560,64,128]{2,1,0:T(8,128)} async-done(((f32[80,64,128]{2,1,0:T(8,128)}), f32[2560,64,128]{2,1,0:T(8,128)}) %all-gather.4.cloned.1.call-update) | async-done | bytes 83886096 | tf_op jit(solution)/shard_map/all_gather | solution.py:23
  286.3 74.3 %while.18 = (s32[]{:T(128)}, f32[80,64,128]{2,1,0:T(8,128)S(1)}, s32[]{:T(128)}, f32[32,80]{1,0:T(8,128)S(1)}, f32[32,80,64,128]{3,2,1,0:T(8,128)}, /*index=5*/s32[]{:T(128)}, s32[]{:T(128)}) while((s32[]{:T(128)}, f32[80,64,128]{2,1,0:T(8,128)S(1)}, s32[]{:T(128)}, f32[32,80]{1,0:T(8,128)S(1)}, f32[32,80,64,128]{3,2,1,0:T(8,128)}, ...), condition=%wide.region_5.6_spmd.clone, body=%wide.region_4.5_spmd.clone.sunk | while | flops 2621444 | bytes 7865385 | solution.py:32
  288.7 2.4 fusion.71
  291.1 2.4 fusion.71
  293.5 2.4 fusion.71
  295.9 2.4 fusion.71
  298.3 2.4 fusion.71
  303.1 2.4 fusion.71
  305.5 2.4 fusion.71
  307.9 2.4 fusion.71
  310.3 2.4 fusion.71
  312.7 2.4 fusion.71
  315.1 2.4 fusion.71
  317.5 2.4 fusion.71
  319.9 2.4 fusion.71
  322.3 2.4 fusion.71
  324.7 2.4 fusion.71
  329.5 2.4 fusion.71
  331.9 2.4 fusion.71
  334.3 2.4 fusion.71
  336.7 2.4 fusion.71
  339.1 2.4 fusion.71
  341.5 2.4 fusion.71
  343.9 2.4 fusion.71
  348.7 2.4 fusion.71
  351.1 2.4 fusion.71
  353.5 2.4 fusion.71
  360.6 3.5 add_select_fusion
  364.2 5.4 %fusion.37 = f32[256,80,64]{0,2,1:T(8,128)} fusion(f32[80,64,128]{2,1,0:T(8,128)S(1)} %get-tuple-element.138, bf16[256,5376]{1,0:T(8,128)(2,1)} %copy-done.1), kind=kOutput, calls=%fused_computation.76 | convolution fusion | flops 2013265920 | bytes 7929856 | tf_op jit(solution)/shard_map/tn,hpn->thp/dot_general | solution.py:74
  371.3 7.4 %fusion.9 = f32[256,80,64]{0,2,1:T(8,128)} fusion(f32[128,80,64]{0,2,1:T(8,128)S(1)} %copy-done.5, f32[128,80,64]{0,2,1:T(8,128)} %fusion.33, f32[256,80,64]{0,2,1:T(8,128)} %bitcast.82, f32[256,80,64]{0,2,1:T(8,128)} %fusion.37, f32[80]{0:T(128)S(1)} %copy-done.16, f32[256,80]{0,1:T(8,128)S(1)} %exponential_bitcast_fusion), kind=kLoop, calls=%fused_computation.19 | loop fusion | flops 6553600 | bytes 21053760 | tf_op jit(solution)/shard_map/add | solution.py:111
  378.7 6.3 %copy.72 = f32[256,5120]{1,0:T(8,128)} copy(f32[256,5120]{0,1:T(8,128)} %bitcast.83) | data formatting | bytes 10485760 | tf_op jit(solution)/shard_map/reshape | solution.py:111
  385.0 4.4 multiply_reduce_fusion
  389.4 3.2 multiply_convert_fusion.1
  392.6 95.8 %all-reduce.4.cloned.1.call-done = f32[80,64,128]{2,1,0:T(8,128)} async-done(((f32[80,64,128]{2,1,0:T(8,128)}), f32[80,64,128]{2,1,0:T(8,128)}) %all-reduce.4.cloned.1.call-update) | async-done | bytes 2621456 | tf_op jit(solution)/shard_map/psum | solution.py:37
  488.5 3.1 fusion.44
  491.6 4.1 multiply_reduce_fusion.1
  497.9 3.4 broadcast_select_fusion
  (120 shorter events, 47.8 us)
Async XLA Ops:
  7.2 279.1 %all-gather.4.cloned.1.call-start = ((), (), s32[]{:S(2)}) async-start(), calls=%async_computation.1 | async-start | bytes 86507520 | tf_op jit(solution)/shard_map/all_gather | solution.py:23
  8.1 6.0 %collective-permute-start = (bf16[3,5376]{1,0:T(4,128)(2,1)S(1)}, bf16[3,5376]{1,0:T(4,128)(2,1)S(1)}, u32[]{:S(2)}, u32[]{:S(2)}) collective-permute-start(bf16[3,5376]{1,0:T(4,128)(2,1)S(1)} %slice.129), channel_id=1, source_target_pairs={{0,1},{1,2},{2,3},{3,4},{4,5},{5,6},{6,7},{7,8},{8,9},{9,10},{10,1... | collective-permute-start | bytes 96776 | tf_op jit(solution)/shard_map/ppermute | solution.py:18
  14.1 2.4 copy-start.12
  20.0 8.8 %copy-start.1 = (bf16[256,5376]{1,0:T(8,128)(2,1)}, bf16[256,5376]{1,0:T(8,128)(2,1)S(1)}, u32[]{:S(2)}) copy-start(bf16[256,5376]{1,0:T(8,128)(2,1)S(1)} %multiply_convert_fusion) | copy-start | bytes 8257540
  26.9 3.4 copy-start.8
  28.8 1.5 copy-start.2
  32.3 0.9 copy-start.11
  32.3 1.8 copy-start.17
  32.4 456.1 %all-reduce.4.cloned.1.call-start = ((), (), s32[]{:S(2)}) async-start(), calls=%async_computation | async-start | bytes 5242880 | tf_op jit(solution)/shard_map/psum | solution.py:37
  155.6 1.1 copy-start.6
  156.7 3.6 copy-start.14
  160.4 3.9 copy-start.15
  178.3 4.0 copy-start.7
  182.3 3.6 copy-start.3
  369.5 1.7 copy-start.5
  369.5 1.7 copy-start.16
  378.7 6.3 %copy-start.4 = (bf16[256,5120]{1,0:T(8,128)(2,1)S(1)}, bf16[256,5120]{1,0:T(8,128)(2,1)}, u32[]{:S(2)}) copy-start(bf16[256,5120]{1,0:T(8,128)(2,1)} %param.16) | copy-start | bytes 7864324
  385.0 4.4 copy-start
  385.0 4.4 copy-start.13
  392.6 99.0 %copy-start.9 = (f32[1,128,5120]{1,2,0:T(8,128)S(1)}, f32[1,128,5120]{1,2,0:T(8,128)}, u32[]{:S(2)}) copy-start(f32[1,128,5120]{1,2,0:T(8,128)} %copy.78) | copy-start | bytes 7864324
  488.5 3.2 copy-start.10
Sparse Core Ops, SparseCore 0:
  32.5 253.7 all-gather.3
  369.7 118.7 all-reduce.3
where the time goes:
time: 511 us; the launch traced here: 508 us
  waiting for transfers between devices  193 us (38%)
  blocking collectives  115 us (23%)
  other arithmetic  112 us (22%)
  local copies, waits for them, and re-layouts  38.4 us (8%)
  matrix products  30.6 us (6%)
  between operations  15.6 us (3%)
    unnamed x1, blocking collectives  115 us
    all_gather x1, waiting for transfers between devices, prefix(): pieces = jax.tree.map(lambda part: lax.all_gather(part, axis), value)  96.8 us
    psum x1, waiting for transfers between devices, from_root(): return lax.psum(block, axis)  95.8 us
    select_n x31, other arithmetic, lap(): jnp.where(position < mine, new, old)  72.9 us
    dot_general x3, matrix products, carried(): jnp.einsum('tn,hpn->thp', queries, carry_state, precision=lax.Precision.H...  12.1 us
    dot_general x3, matrix products, block_local(): jnp.einsum('hts,shp->thp', mixing, values, preferred_element_type=jnp.flo...  11.7 us
    slice x5, local copies, waits for them, and re-layouts, block_local(): values = activations[:, :D_INNER].reshape(row_count, HEADS, HEAD_DIM)  10.5 us
  transfers between devices with their start and end apart: 3, of which 2 were waited for; matrix products, arithmetic and copies ran while one was open for 13% of the time, Pallas kernels for 0%

commit v1 on v0

--- a/solution.py
+++ b/solution.py
@@ -34,7 +34,7 @@
 
 def from_root(block, axis, source):
     block = jnp.where(lax.axis_index(axis) == source, block, jnp.zeros_like(block))
-    return lax.psum(block, axis)
+    return jnp.sum(lax.all_gather(block, axis), axis=0)
 
 
 def conv_silu(input_rows, history, conv_weight, conv_bias):

time: 511 us -> 662 us (1.30)
  waiting for transfers between devices: 193 us -> 321 us
  other arithmetic: 112 us -> 139 us
    all_gather x0 -> x2, waiting for transfers between devices: none -> 187 us  [from_root(): return jnp.sum(lax.all_gather(block, axis), axis=0)]
    psum x1 -> x0, waiting for transfers between devices: 95.8 us -> none  [from_root(): return lax.psum(block, axis)]
    all_gather x1, waiting for transfers between devices: 96.8 us -> 134 us  [prefix(): pieces = jax.tree.map(lambda part: lax.all_gather(part, axis), value)]
    reduce_sum x0 -> x2, other arithmetic: none -> 28 us  [from_root(): return jnp.sum(lax.all_gather(block, axis), axis=0)]
  transfers between devices with their start and end apart: 3 -> 4, of which waited for: 2 -> 2; matrix products, arithmetic and copies ran while one was open for 13% -> 22% of each run, Pallas kernels for 0% -> 0%
where the time goes in v1:
time: 662 us; the launch traced here: 658 us
  waiting for transfers between devices  321 us (48%)
  other arithmetic  139 us (21%)
  blocking collectives  115 us (17%)
  local copies, waits for them, and re-layouts  36.3 us (5%)
  matrix products  27.5 us (4%)
  between operations  15.5 us (2%)
    all_gather x2, waiting for transfers between devices, from_root(): return jnp.sum(lax.all_gather(block, axis), axis=0)  187 us
    all_gather x1, waiting for transfers between devices, prefix(): pieces = jax.tree.map(lambda part: lax.all_gather(part, axis), value)  134 us
    unnamed x1, blocking collectives  115 us
    select_n x31, other arithmetic, lap(): jnp.where(position < mine, new, old)  73.4 us
    reduce_sum x2, other arithmetic, from_root(): return jnp.sum(lax.all_gather(block, axis), axis=0)  28 us
  transfers between devices with their start and end apart: 4, of which 2 were waited for; matrix products, arithmetic and copies ran while one was open for 22% of the time, Pallas kernels for 0%

profile of v1, /device:TPU:6, one launch (start us, length us, event | category | flops | bytes accessed | tf_op | source)
XLA Modules:
  0.0 657.8 jit_solution(7899771135702684344)
XLA Ops:
  16.5 3.5 multiply_convert_fusion
  22.0 2.4 copy.60
  24.4 2.4 copy.61
  36.8 115.2 %all-reduce = f32[2560]{0:T(1024)S(1)} all-reduce(f32[2560]{0:T(1024)S(1)} %dynamic-update-slice), channel_id=2, replica_groups=mesh['grp'=8,'seq'=16,'resp'=2] {'seq','resp'}, use_global_device_ids=true, to_apply=%add | all-reduce | flops 2560 | bytes 20480
  152.1 134.2 %all-gather.9.cloned.1.call-done = f32[2560,64,128]{2,1,0:T(8,128)} async-done(((f32[80,64,128]{2,1,0:T(8,128)}), f32[2560,64,128]{2,1,0:T(8,128)}) %all-gather.9.cloned.1.call-update) | async-done | bytes 83886096 | tf_op jit(solution)/shard_map/all_gather | solution.py:23
  286.3 74.8 %while.18 = (s32[]{:T(128)}, f32[80,64,128]{2,1,0:T(8,128)S(1)}, s32[]{:T(128)}, f32[32,80]{1,0:T(8,128)S(1)}, f32[32,80,64,128]{3,2,1,0:T(8,128)}, /*index=5*/s32[]{:T(128)}, s32[]{:T(128)}) while((s32[]{:T(128)}, f32[80,64,128]{2,1,0:T(8,128)S(1)}, s32[]{:T(128)}, f32[32,80]{1,0:T(8,128)S(1)}, f32[32,80,64,128]{3,2,1,0:T(8,128)}, ...), condition=%wide.region_5.6_spmd.clone, body=%wide.region_4.5_spmd.clone.sunk | while | flops 2621444 | bytes 7865385 | solution.py:32
  288.7 2.4 fusion.71
  291.1 2.4 fusion.71
  293.5 2.4 fusion.71
  295.9 2.4 fusion.71
  298.3 2.4 fusion.71
  300.7 2.4 fusion.71
  303.1 2.4 fusion.71
  305.5 2.4 fusion.71
  307.9 2.4 fusion.71
  310.4 2.4 fusion.71
  312.8 2.4 fusion.71
  319.9 2.4 fusion.71
  322.3 2.6 fusion.71
  325.0 2.4 fusion.71
  327.4 2.5 fusion.71
  329.9 2.4 fusion.71
  332.3 2.4 fusion.71
  334.7 2.4 fusion.71
  337.1 2.4 fusion.71
  339.5 2.4 fusion.71
  341.9 2.4 fusion.71
  344.3 2.4 fusion.71
  346.7 2.4 fusion.71
  349.1 2.4 fusion.71
  351.5 2.4 fusion.71
  361.1 3.5 add_select_fusion
  365.7 2.8 copy.75
  369.3 4.7 slice_convert_fusion
  374.0 6.3 copy.68
  382.2 4.0 fusion.15
  386.2 3.6 fusion.33
  389.8 3.6 bitcast_add_fusion.2
  401.4 2.4 copy.70
  404.8 3.2 fusion.37
  408.1 5.2 fusion.9
  413.3 6.1 copy.69
  419.4 4.3 multiply_reduce_fusion
  423.7 3.0 multiply_convert_fusion.1
  426.7 186.9 %all-gather.11.cloned.1.call-done = f32[2560,64,128]{2,1,0:T(8,128)} async-done(((f32[80,64,128]{2,1,0:T(8,128)}), f32[2560,64,128]{2,1,0:T(8,128)}) %all-gather.11.cloned.1.call-update) | async-done | bytes 83886096 | tf_op jit(solution)/shard_map/all_gather | solution.py:37
  613.6 25.8 %reduce_sum.39 = f32[80,64,128]{2,1,0:T(8,128)S(1)} reduce(f32[32,80,64,128]{3,2,1,0:T(8,128)} %bitcast.26, f32[]{:T(128)} %constant.79.clone.1), dimensions={0}, to_apply=%region_9.10 | reduce | flops 20316160 | bytes 86507520 | tf_op jit(solution)/shard_map/reduce_sum | solution.py:37
  641.6 4.1 multiply_reduce_fusion.1
  647.9 3.4 broadcast_select_fusion
  (127 shorter events, 51.2 us)
Async XLA Ops:
  7.2 279.1 %all-gather.9.cloned.1.call-start = ((), (), s32[]{:S(2)}) async-start(), calls=%async_computation | async-start | bytes 86507520 | tf_op jit(solution)/shard_map/all_gather | solution.py:23
  8.1 6.0 collective-permute-start
  14.1 2.4 copy-start.13
  20.0 8.8 %copy-start.1 = (bf16[256,5376]{1,0:T(8,128)(2,1)}, bf16[256,5376]{1,0:T(8,128)(2,1)S(1)}, u32[]{:S(2)}) copy-start(bf16[256,5376]{1,0:T(8,128)(2,1)S(1)} %multiply_convert_fusion) | copy-start | bytes 8257540
  26.8 3.4 copy-start.8
  28.8 1.5 copy-start.2
  32.3 1.7 copy-start.12
  32.3 2.9 copy-start.18
  32.3 361.1 %all-gather.13.cloned.1.call-start = ((), (), s32[]{:S(2)}) async-start(), calls=%async_computation.2 | async-start | bytes 2838528 | tf_op jit(solution)/shard_map/all_gather | solution.py:37
  34.0 579.6 %all-gather.11.cloned.1.call-start = ((), (), s32[]{:S(2)}) async-start(), calls=%async_computation.1 | async-start | bytes 86507520 | tf_op jit(solution)/shard_map/all_gather | solution.py:37
  364.6 0.8 copy-start.15
  364.6 4.6 copy-start.16
  382.2 4.0 copy-start.7
  386.2 3.6 copy-start.3
  399.2 1.1 copy-start.6
  404.8 3.3 copy-start.5
  404.8 3.3 copy-start.10
  404.8 3.3 copy-start.17
  413.3 6.1 copy-start.4
  419.4 4.3 copy-start
  419.4 4.3 copy-start.14
  639.4 2.2 copy-start.9
  639.4 2.2 copy-start.11
Sparse Core Ops, SparseCore 0:
  32.4 253.7 all-gather.8
  288.9 48.4 all-gather.12
  364.7 248.8 all-gather.10
